TPU v7x, 32 devices: a whole 2x2x4 slice. The times are simulated.
32 devices in a mesh: groups: 2 (over x), row: 16 (over z, y, core).
Axes of the slice: x: 2, y: 2, z: 4, core: 2. Of those that a mesh axis runs over, the one named last changes fastest.
Arguments:
- basis: float32 [8192, 128], P(('groups', 'row')), parts along dimension 0, may hold values from -6 to 6
- springs: float32 [8192], P(('groups', 'row')), parts along dimension 0, may hold values from 0.25 to 8
- tangent_blocks: float32 [4096, 4096], P(('groups', 'row')), parts along dimension 0, may hold values from -0.375 to 0.375
- tile_rows: int32 [4096], P(('groups', 'row')), parts along dimension 0, may hold values from 0 to 3
- tile_owner: int32 [4096, 1], P(('groups', 'row')), parts along dimension 0, may hold values from 0 to 15, as said below
- tile_offset: int32 [4096], P(('groups', 'row')), parts along dimension 0, may hold values from 0 to 3
- tile_count: int32 [32], P(('groups', 'row')), parts along dimension 0, may hold values from 32 to 128, as said below
Outputs:
- stiff_image: float32 [8192, 128], P(('groups', 'row')), parts along dimension 0
- reduced: float32 [256, 128], P('groups'), parts along dimension 0
There are 2 independent parts, one for each index of `groups`. A program takes and returns all parts, laid end to end along the dimension named above; each array names one. Nothing has to cross between parts.
Inputs may be any that keep to these rules, and one draw needn't show every extreme that they name: The first tile_count[d] slots of device d are live; some device has exactly 128. `tile_owner`: the slab is closed into a shell: every slot of device d names owner (d + o) mod 16 with o one of 0, 1, -1, 4, -4, 5, -5, 8. Among the slots of one device no owner appears more than 32 times, and owner d itself appears exactly 32 times in every device.
All inputs are finite; a program needn't handle non-finite values.
Results may differ from a plain program's by a relative error of at most 0.0003.
Values sent between devices are 32-bit elements; how exact they have to be, the bound alone decides.
A program may use at most 128 MiB of HBM per device.

v0:
```python
import jax
import jax.numpy as jnp
from jax import lax
from jax.sharding import PartitionSpec as P

B = 64
MODES = 128
BR_DEV = 4
CAP = 128


def shards(basis, springs, tangent_blocks, tile_rows, tile_owner, tile_offset, tile_count):
    row_devices = lax.axis_size("row")
    dof_total = basis.shape[0] * row_devices
    own_blocks = basis.reshape(BR_DEV, B, MODES)
    square_blocks = tangent_blocks.reshape(CAP, B, B)
    owner_ids = tile_owner[:, 0]
    gathered = lax.all_gather(own_blocks, "row", axis=0, tiled=True)
    picked = gathered[owner_ids * BR_DEV + tile_offset]
    live_slot = (jnp.arange(CAP, dtype=jnp.int32) < tile_count[0]).astype(jnp.float32)
    row_ids = jnp.arange(BR_DEV, dtype=jnp.int32)
    products = jnp.einsum("sij,sjk->sik", square_blocks, picked, precision=lax.Precision.HIGHEST)
    row_select = (tile_rows[None, :] == row_ids[:, None]).astype(jnp.float32) * live_slot[None, :]
    summed = jnp.dot(row_select, products.reshape(CAP, B * MODES), precision=lax.Precision.HIGHEST)
    stiff_image = springs[:, None] * basis + summed.reshape(BR_DEV * B, MODES)
    partial_term = (
        jnp.einsum("rm,rn->mn", basis, stiff_image, precision=lax.Precision.HIGHEST) / dof_total
    )
    reduced = lax.psum(partial_term, "row")
    return (stiff_image, reduced)


def solution(mesh):
    in_specs = (
        P(("groups", "row"), None),
        P(("groups", "row")),
        P(("groups", "row"), None),
        P(("groups", "row")),
        P(("groups", "row"), None),
        P(("groups", "row")),
        P(("groups", "row")),
    )
    out_specs = (P(("groups", "row"), None), P("groups", None))
    return jax.shard_map(shards, mesh=mesh, in_specs=in_specs, out_specs=out_specs, check_vma=False)
```

profile of v0, /device:TPU:0, one launch (start us, length us, event | category | flops | bytes accessed | tf_op | source)
XLA Modules:
  0.0 162.7 jit_solution(6896301566178183216)
XLA Ops:
  7.2 0.0 all-gather.2.cloned.1.call-start
  7.2 0.7 all-gather.2.cloned.1.call-update
  7.9 0.0 all-reduce.2.cloned.1.call-start
  7.9 1.9 %copy.13 = f32[128,4096]{0,1:T(8,128)S(1)} copy(f32[128,4096]{1,0:T(8,128)} %param.9) | data formatting | bytes 4194304 | tf_op args[2]
  9.9 0.0 copy-start.4
  9.9 0.0 copy-start.5
  9.9 4.5 %copy.14 = f32[128,64,64]{2,1,0:T(8,128)} copy(f32[128,64,64]{0,2,1:T(8,128)S(1)} %bitcast.20) | data formatting | bytes 4194304 | tf_op jit(solution)/shard_map/reshape | solution.py:16
  15.1 0.0 copy-done.4
  15.1 0.0 copy-done.5
  15.1 39.2 %all-gather.2.cloned.1.call-done = f32[64,64,128]{2,1,0:T(8,128)} async-done(((f32[4,64,128]{2,1,0:T(8,128)}), f32[64,64,128]{2,1,0:T(8,128)}) %all-gather.2.cloned.1.call-update) | async-done | bytes 2097168 | tf_op jit(solution)/shard_map/all_gather | solution.py:18
  54.3 4.4 %gather_fusion = f32[128,64,128]{2,1,0:T(8,128)} fusion(f32[64,64,128]{2,1,0:T(8,128)} %all-gather.2.cloned.1.call-done, s32[1024]{0:T(1024)S(1)} %pad_clamp_fusion), kind=kCustom, calls=%fused_computation | custom fusion | bytes 8389120 | tf_op jit(solution)/shard_map/gather | solution.py:19
  58.6 0.0 copy-start.3
  58.6 6.5 %fusion.9 = f32[128,128,64]{1,2,0:T(8,128)S(1)} fusion(f32[128,64,128]{2,1,0:T(8,128)} %gather_fusion, f32[128,64,64]{2,1,0:T(8,128)} %copy.14), kind=kOutput, calls=%fused_computation.17 | convolution fusion | flops 805306368 | bytes 10485760 | tf_op jit(solution)/shard_map/sij,sjk->sik/dot_general | solution.py:22
  65.2 0.0 copy-start
  65.2 0.0 copy-start.2
  65.2 0.0 copy-done.3
  65.2 4.3 %fusion = f32[4,8192]{1,0:T(4,128)S(1)} fusion(f32[16,8,64,128]{3,2,1,0:T(8,128)S(1)} %bitcast.19, f32[128]{0:T(128)S(1)} %compare_convert_fusion, s32[128]{0:T(128)S(1)} %copy-done.3), kind=kOutput, calls=%fused_computation.1 | convolution fusion | flops 50332672 | bytes 4326400 | tf_op jit(solution)/shard_map/dot_general | solution.py:24
  69.6 0.1 reshape.28
  69.7 0.0 copy-done
  69.7 0.0 copy-done.2
  69.7 0.1 multiply_add_fusion
  69.8 0.0 copy-start.1
  69.8 1.0 fusion.3
  70.8 0.0 all-reduce.2.cloned.1.call-update
  70.8 83.4 %all-reduce.2.cloned.1.call-done = f32[128,128]{0,1:T(8,128)} async-done(((f32[128,128]{0,1:T(8,128)}), f32[128,128]{0,1:T(8,128)}) %all-reduce.2.cloned.1.call-update) | async-done | bytes 65552 | tf_op jit(solution)/shard_map/psum | solution.py:29
  154.2 1.6 copy.15
  155.8 0.0 copy-done.1
  (3 shorter events, 0.0 us)
Async XLA Ops:
  7.2 47.1 %all-gather.2.cloned.1.call-start = ((), (), s32[]{:S(2)}) async-start(), calls=%async_computation | async-start | bytes 2228224 | tf_op jit(solution)/shard_map/all_gather | solution.py:18
  7.9 146.3 %all-reduce.2.cloned.1.call-start = ((), (), s32[]{:S(2)}) async-start(), calls=%async_computation.1 | async-start | bytes 131072 | tf_op jit(solution)/shard_map/psum | solution.py:29
  9.9 5.2 %copy-start.4 = (s32[128]{0:T(128)S(1)}, s32[128]{0:T(128)}, u32[]{:S(2)}) copy-start(s32[128]{0:T(128)} %param.12) | copy-start | bytes 1540
  9.9 5.2 %copy-start.5 = (s32[128,1]{0,1:T(1,128)S(1)}, s32[128,1]{0,1:T(1,128)}, u32[]{:S(2)}) copy-start(s32[128,1]{0,1:T(1,128)} %param.11) | copy-start | bytes 1540
  58.6 6.6 %copy-start.3 = (s32[128]{0:T(128)S(1)}, s32[128]{0:T(128)}, u32[]{:S(2)}) copy-start(s32[128]{0:T(128)} %param.10) | copy-start | bytes 1540
  65.2 4.5 %copy-start = (f32[256,128]{1,0:T(8,128)S(1)}, f32[256,128]{1,0:T(8,128)}, u32[]{:S(2)}) copy-start(f32[256,128]{1,0:T(8,128)} %param.7) | copy-start | bytes 393220
  65.2 4.5 %copy-start.2 = (f32[256]{0:T(256)S(1)}, f32[256]{0:T(256)}, u32[]{:S(2)}) copy-start(f32[256]{0:T(256)} %param.8) | copy-start | bytes 3076
  69.8 86.0 %copy-start.1 = (f32[256,128]{1,0:T(8,128)}, f32[256,128]{1,0:T(8,128)S(1)}, u32[]{:S(2)}) copy-start(f32[256,128]{1,0:T(8,128)S(1)} %multiply_add_fusion) | copy-start | bytes 393220
Sparse Core Ops, SparseCore 0:
  10.2 44.0 all-gather.1
  71.0 83.2 all-reduce.1
where the time goes:
time: 164 us; the launch traced here: 163 us
  waiting for transfers between devices  123 us (75%)
  between operations  14.8 us (9%)
  local copies, waits for them, and re-layouts  12.5 us (8%)
  matrix products  11.9 us (7%)
    psum x1, waiting for transfers between devices, shards(): reduced = lax.psum(partial_term, 'row')  83.4 us
    all_gather x1, waiting for transfers between devices, shards(): gathered = lax.all_gather(own_blocks, 'row', axis=0, tiled=True)  39.2 us
    dot_general x1, matrix products, shards(): jnp.einsum('sij,sjk->sik', square_blocks, picked, precision=lax.Precision...  6.52 us
    reshape x1, local copies, waits for them, and re-layouts, shards(): square_blocks = tangent_blocks.reshape(CAP, B, B)  4.52 us
    gather x1, local copies, waits for them, and re-layouts, shards(): picked = gathered[owner_ids * BR_DEV + tile_offset]  4.35 us
    dot_general x1, matrix products, shards(): jnp.dot(row_select, products.reshape(CAP, B * MODES), precision=lax.Preci...  4.34 us
    unnamed x14, local copies, waits for them, and re-layouts  3.52 us
  transfers between devices with their start and end apart: 2, of which 2 were waited for; matrix products, arithmetic and copies ran while one was open for 4% of the time, Pallas kernels for 0%

commit v1 on v0

v1 whole, which is shorter than its diff:
```python
import functools

import jax
import jax.numpy as jnp
from jax import lax
from jax.experimental import pallas as pl
from jax.experimental.pallas import tpu as pltpu
from jax.sharding import PartitionSpec as P

B = 64
MODES = 128
BR_DEV = 4
CAP = 128
SUB = 16
F32, BF16 = jnp.float32, jnp.bfloat16


def split(x):
    hi = x.astype(BF16)
    return hi, (x - hi.astype(F32)).astype(BF16)


def mm(a, b):
    return jnp.dot(a, b, preferred_element_type=F32)


def mm3(a_hi, a_lo, b_hi, b_lo):
    both = mm(a_hi, jnp.concatenate([b_hi, b_lo], axis=1))
    return both[:, :MODES] + both[:, MODES:] + mm(a_lo, b_hi)


def kernel(
    n, dof_total,
    basis, springs, tangent, rows, owner, offset, count,
    stiff, reduced,
    shard, tang, dense_hi, dense_lo, acc, part, rs_buf, top_buf, red,
    loc_sem, send_sem, recv_sem, rs_send, rs_recv, top_send, top_recv, ag_send, ag_recv,
):
    me = lax.axis_index("row")
    steps = (0, 1, n - 1, 4, n - 4, 5, n - 5, n // 2)
    subs = n // SUB
    sub, pos = me // SUB, me % SUB

    def at(p):
        return {"row": p}

    def mate(s):
        return sub * SUB + (pos + s) % SUB

    barrier = pltpu.get_barrier_semaphore()
    greeted = [mate(s) for s in range(1, SUB)]
    if subs > 1:
        greeted += [(me + o) % n for o in steps[1:]] + [(me + SUB * q) % n for q in range(1, subs)]
    for p in greeted:
        pl.semaphore_signal(barrier, inc=1, device_id=at(p), device_id_type=pl.DeviceIdType.MESH)
    own_copy = pltpu.make_async_copy(basis, shard.at[0], loc_sem.at[0])
    own_copy.start()
    tang_copy = pltpu.make_async_copy(tangent, tang, loc_sem.at[1])
    tang_copy.start()
    pl.semaphore_wait(barrier, len(greeted))

    sends = []
    for k in (7, 5, 6, 3, 4, 1, 2):
        c = pltpu.make_async_remote_copy(
            basis, shard.at[k], send_sem.at[k], recv_sem.at[k],
            device_id=at((me + n - steps[k]) % n), device_id_type=pl.DeviceIdType.MESH,
        )
        c.start()
        sends.append((k, c))

    away = owner[...] - me
    away = jnp.where(away < 0, away + n, away)
    key = jnp.zeros_like(away)
    for k in range(1, 8):
        key = jnp.where(away == steps[k], k, key)
    place = key * 16 + offset[...] * 4 + rows[...]
    slot = lax.broadcasted_iota(jnp.int32, (1, CAP), 1)
    place = jnp.where(slot < count[0], place, -1)
    p_ids = lax.broadcasted_iota(jnp.int32, (CAP, CAP), 0)
    lane = lax.broadcasted_iota(jnp.int32, (CAP, CAP), 1)
    swapped = jnp.where((p_ids // 4) % 2 == 0, p_ids + 4, p_ids - 4)
    hot = jnp.concatenate([(p_ids == place), (swapped == place)], axis=0)
    hot = jnp.where(hot, 1.0, 0.0).astype(BF16)
    hot = jnp.concatenate([hot, hot], axis=1)
    keep = (p_ids // 4) % 2 == lane // B

    tang_copy.wait()

    def build(it, _):
        t = tang[:, pl.ds(pl.multiple_of(it * 256, 256), 256)]
        t_hi, t_lo = split(t)
        e = mm(hot, jnp.concatenate([t_hi, t_lo], axis=0))
        out = []
        for m in range(2):
            a = e[:CAP, m * 128:(m + 1) * 128]
            b = pltpu.roll(e[CAP:, m * 128:(m + 1) * 128], B, 1)
            out.append(jnp.where(keep, a, b))
        at_row = pl.ds(pl.multiple_of(it * 16, 16), 16)
        for cp in range(16):
            x = jnp.concatenate([out[0][cp * 8:cp * 8 + 8], out[1][cp * 8:cp * 8 + 8]], axis=0)
            hi, lo = split(x)
            dense_hi[at_row, cp * 128:(cp + 1) * 128] = hi
            dense_lo[at_row, cp * 128:(cp + 1) * 128] = lo
        return 0

    lax.fori_loop(0, 16, build, 0)

    own_copy.wait()
    own = shard[0]
    t_hi, t_lo = split(own.T)
    eye = p_ids == lane
    spring = jnp.concatenate(
        [jnp.sum(jnp.where(eye, springs[h:h + 1, :], 0.0), axis=1, keepdims=True) for h in range(2)], axis=0
    )
    scaled = spring * own

    def term(k, g):
        g_hi, g_lo = split(g)
        ks = slice(k * 256, (k + 1) * 256)
        return mm3(dense_hi[:, ks], dense_lo[:, ks], g_hi, g_lo)

    total = term(0, own)
    for k in (1, 2, 3, 4, 5, 6, 7):
        pltpu.make_async_copy(shard.at[k], shard.at[k], recv_sem.at[k]).wait()
        total = total + term(k, shard[k])
    acc[...] = total
    image = scaled + jnp.concatenate([acc[pl.ds(r, B, stride=BR_DEV), :] for r in range(BR_DEV)], axis=0)
    stiff[...] = image
    i_hi, i_lo = split(image)
    part[...] = (mm3(t_hi, t_lo, i_hi, i_lo) * (1.0 / dof_total)).reshape(SUB, 8, MODES)

    rs = []
    for s in range(1, SUB):
        c = pltpu.make_async_remote_copy(
            part.at[(pos + s) % SUB], rs_buf.at[s], rs_send.at[s], rs_recv.at[s],
            device_id=at(mate(s)), device_id_type=pl.DeviceIdType.MESH,
        )
        c.start()
        rs.append(c)
    mine = part[pos]
    for s in range(1, SUB):
        rs[s - 1].wait_recv()
        mine = mine + rs_buf[s]
    if subs > 1:
        top_buf[sub] = mine
        top = []
        for q in range(1, subs):
            c = pltpu.make_async_remote_copy(
                top_buf.at[sub], top_buf.at[sub], top_send.at[q], top_recv.at[q],
                device_id=at((me + SUB * q) % n), device_id_type=pl.DeviceIdType.MESH,
            )
            c.start()
            top.append(c)
        for c in top:
            c.wait_recv()
        mine = top_buf[0]
        for q in range(1, subs):
            mine = mine + top_buf[q]
    red[pos] = mine
    ag = []
    for s in range(1, SUB):
        c = pltpu.make_async_remote_copy(
            red.at[pos], red.at[pos], ag_send.at[s], ag_recv.at[s],
            device_id=at(mate(s)), device_id_type=pl.DeviceIdType.MESH,
        )
        c.start()
        ag.append(c)
    for c in ag:
        c.wait_recv()
    reduced[...] = red[...].reshape(MODES, MODES)
    for k, c in sends:
        c.wait_send()
    for c in rs + ag:
        c.wait_send()
    if subs > 1:
        for c in top:
            c.wait_send()


def shards(basis, springs, tangent_blocks, tile_rows, tile_owner, tile_offset, tile_count):
    n = lax.axis_size("row")
    dof_total = basis.shape[0] * n
    vm = pl.BlockSpec(memory_space=pltpu.VMEM)
    hbm = pl.BlockSpec(memory_space=pl.ANY)
    subs = max(n // SUB, 2)
    return pl.pallas_call(
        functools.partial(kernel, n, dof_total),
        out_shape=(
            jax.ShapeDtypeStruct((BR_DEV * B, MODES), F32),
            jax.ShapeDtypeStruct((MODES, MODES), F32),
        ),
        in_specs=[hbm, vm, hbm, vm, vm, vm, pl.BlockSpec(memory_space=pltpu.SMEM)],
        out_specs=(vm, vm),
        scratch_shapes=[
            pltpu.VMEM((8, BR_DEV * B, MODES), F32),
            pltpu.VMEM((CAP, B * B), F32),
            pltpu.VMEM((BR_DEV * B, 32 * B), BF16),
            pltpu.VMEM((BR_DEV * B, 32 * B), BF16),
            pltpu.VMEM((BR_DEV * B, MODES), F32),
            pltpu.VMEM((SUB, 8, MODES), F32),
            pltpu.VMEM((SUB, 8, MODES), F32),
            pltpu.VMEM((subs, 8, MODES), F32),
            pltpu.VMEM((SUB, 8, MODES), F32),
            pltpu.SemaphoreType.DMA((2,)),
            pltpu.SemaphoreType.DMA((8,)),
            pltpu.SemaphoreType.DMA((8,)),
            pltpu.SemaphoreType.DMA((SUB,)),
            pltpu.SemaphoreType.DMA((SUB,)),
            pltpu.SemaphoreType.DMA((subs,)),
            pltpu.SemaphoreType.DMA((subs,)),
            pltpu.SemaphoreType.DMA((SUB,)),
            pltpu.SemaphoreType.DMA((SUB,)),
        ],
        compiler_params=pltpu.CompilerParams(
            collective_id=0, has_side_effects=True, vmem_limit_bytes=32 * 1024 * 1024
        ),
    )(
        basis, springs.reshape(2, MODES), tangent_blocks,
        tile_rows.reshape(1, CAP), tile_owner.reshape(1, CAP), tile_offset.reshape(1, CAP), tile_count,
    )


def solution(mesh):
    in_specs = (
        P(("groups", "row"), None),
        P(("groups", "row")),
        P(("groups", "row"), None),
        P(("groups", "row")),
        P(("groups", "row"), None),
        P(("groups", "row")),
        P(("groups", "row")),
    )
    out_specs = (P(("groups", "row"), None), P("groups", None))
    return jax.shard_map(shards, mesh=mesh, in_specs=in_specs, out_specs=out_specs, check_vma=False)
```

time: 164 us -> 45.1 us (0.28)
  waiting for transfers between devices: 123 us -> 0 us
  Pallas kernels: 0 us -> 37.2 us
  between operations: 14.8 us -> 1.3 us
  matrix products: 11.9 us -> 0 us
  local copies, waits for them, and re-layouts: 12.5 us -> 6.42 us
    psum x1 -> x0, waiting for transfers between devices: 83.4 us -> none  [shards(): reduced = lax.psum(partial_term, 'row')]
    all_gather x1 -> x0, waiting for transfers between devices: 39.2 us -> none  [shards(): gathered = lax.all_gather(own_blocks, 'row', axis=0, tiled=True)]
    pallas_call x0 -> x1, Pallas kernels: none -> 37.2 us  [shards(): pl.pallas_call(functools.partial(kernel, n, dof_total), out_shape=(jax.Sh...]
    dot_general x3 -> x0, matrix products: 11.9 us -> none  [the longest x1 6.52 us: shards(): jnp.einsum('sij,sjk->sik', square_blocks, picked, precision=lax.Precision...]
    reshape x2 -> x0, local copies, waits for them, and re-layouts: 4.62 us -> none  [the longest x1 4.52 us: shards(): square_blocks = tangent_blocks.reshape(CAP, B, B)]
    gather x1 -> x0, local copies, waits for them, and re-layouts: 4.35 us -> none  [shards(): picked = gathered[owner_ids * BR_DEV + tile_offset]]
    unnamed x14, local copies, waits for them, and re-layouts: 3.52 us -> 6.42 us
  transfers between devices with their start and end apart: 2 -> 0, of which waited for: 2 -> 0; matrix products, arithmetic and copies ran while one was open for 4% -> 0% of each run, Pallas kernels for 0% -> 0%
where the time goes in v1:
time: 45.1 us; the launch traced here: 44.9 us
  Pallas kernels  37.2 us (82%)
  local copies, waits for them, and re-layouts  6.42 us (14%)
  between operations  1.3 us (3%)
    pallas_call x1, Pallas kernels, shards(): pl.pallas_call(functools.partial(kernel, n, dof_total), out_shape=(jax.Sh...  37.2 us
    unnamed x14, local copies, waits for them, and re-layouts  6.42 us

profile of v1, /device:TPU:0, one launch (start us, length us, event | category | flops | bytes accessed | tf_op | source)
XLA Modules:
  0.0 44.9 jit_solution(215891868100560857)
XLA Ops:
  1.3 0.0 copy-start
  1.3 1.6 %copy-done = f32[128,4096]{1,0:T(8,128)S(1)} copy-done((f32[128,4096]{1,0:T(8,128)S(1)}, f32[128,4096]{1,0:T(8,128)}, u32[]{:S(2)}) %copy-start) | copy-done | bytes 2097176
  2.9 0.0 copy-start.1
  2.9 0.9 %copy-done.1 = f32[256,128]{1,0:T(8,128)S(1)} copy-done((f32[256,128]{1,0:T(8,128)S(1)}, f32[256,128]{1,0:T(8,128)}, u32[]{:S(2)}) %copy-start.1) | copy-done | bytes 131096
  3.8 0.0 copy-start.2
  3.8 0.7 %copy-done.2 = f32[256]{0:T(256)S(1)} copy-done((f32[256]{0:T(256)S(1)}, f32[256]{0:T(256)}, u32[]{:S(2)}) %copy-start.2) | copy-done | bytes 1048
  4.5 0.0 copy-start.3
  4.5 0.7 %copy-done.3 = s32[128]{0:T(128)S(1)} copy-done((s32[128]{0:T(128)S(1)}, s32[128]{0:T(128)}, u32[]{:S(2)}) %copy-start.3) | copy-done | bytes 536
  5.1 0.0 copy-start.4
  5.1 0.7 %copy-done.4 = s32[128,1]{0,1:T(1,128)S(1)} copy-done((s32[128,1]{0,1:T(1,128)S(1)}, s32[128,1]{0,1:T(1,128)}, u32[]{:S(2)}) %copy-start.4) | copy-done | bytes 536
  5.8 0.0 copy-start.5
  5.8 0.7 %copy-done.5 = s32[128]{0:T(128)S(1)} copy-done((s32[128]{0:T(128)S(1)}, s32[128]{0:T(128)}, u32[]{:S(2)}) %copy-start.5) | copy-done | bytes 536
  6.4 37.2 %shard_map.86 = (f32[256,128]{1,0:T(8,128)S(1)}, f32[128,128]{1,0:T(8,128)S(1)}) custom-call(f32[256,128]{1,0:T(8,128)S(1)} %copy-done.1, f32[2,128]{1,0:T(2,128)S(1)} %bitcast.4, f32[128,4096]{1,0:T(8,128)S(1)} %copy-done, s32[1,128]{1,0:T(1,128)S(1)} %bitcast.5, s32[1,128]{1,0:T(1,128)S(1)} %bitcast.6, s32[1,128]{1,0:T(1,128)S(1)} %bitcast.7, s32[1]{0:T(128)S(6)} %copy.11.count), custom_call_target="tpu_custom_call" | custom-call | tf_op jit(solution)/shard_map/pallas_call | solution.py:186
  43.6 0.7 %copy.12 = f32[256,128]{1,0:T(8,128)} copy(f32[256,128]{1,0:T(8,128)S(1)} %get-tuple-element.4) | data formatting | bytes 262144
  44.3 0.6 %copy.13 = f32[128,128]{1,0:T(8,128)} copy(f32[128,128]{1,0:T(8,128)S(1)} %get-tuple-element.5) | data formatting | bytes 131072
Async XLA Ops:
  1.3 1.6 %copy-start = (f32[128,4096]{1,0:T(8,128)S(1)}, f32[128,4096]{1,0:T(8,128)}, u32[]{:S(2)}) copy-start(f32[128,4096]{1,0:T(8,128)} %tangent.1) | copy-start | bytes 6291460
  2.9 0.9 %copy-start.1 = (f32[256,128]{1,0:T(8,128)S(1)}, f32[256,128]{1,0:T(8,128)}, u32[]{:S(2)}) copy-start(f32[256,128]{1,0:T(8,128)} %basis.1) | copy-start | bytes 393220
  3.8 0.7 %copy-start.2 = (f32[256]{0:T(256)S(1)}, f32[256]{0:T(256)}, u32[]{:S(2)}) copy-start(f32[256]{0:T(256)} %param.8) | copy-start | bytes 3076
  4.5 0.7 %copy-start.3 = (s32[128]{0:T(128)S(1)}, s32[128]{0:T(128)}, u32[]{:S(2)}) copy-start(s32[128]{0:T(128)} %param.10) | copy-start | bytes 1540
  5.1 0.7 %copy-start.4 = (s32[128,1]{0,1:T(1,128)S(1)}, s32[128,1]{0,1:T(1,128)}, u32[]{:S(2)}) copy-start(s32[128,1]{0,1:T(1,128)} %param.11) | copy-start | bytes 1540
  5.8 0.7 %copy-start.5 = (s32[128]{0:T(128)S(1)}, s32[128]{0:T(128)}, u32[]{:S(2)}) copy-start(s32[128]{0:T(128)} %param.12) | copy-start | bytes 1540

commit v2 on v1

--- a/solution.py
+++ b/solution.py
@@ -31,10 +31,11 @@
 
 def kernel(
     n, dof_total,
-    basis, springs, tangent, rows, owner, offset, count,
+    basis, springs_in, tangent, rows_in, owner_in, offset_in, count,
     stiff, reduced,
+    springs, rows, owner, offset,
     shard, tang, dense_hi, dense_lo, acc, part, rs_buf, top_buf, red,
-    loc_sem, send_sem, recv_sem, rs_send, rs_recv, top_send, top_recv, ag_send, ag_recv,
+    loc_sem, send_sem, recv_sem, up_send, up_recv, down_send, down_recv, rs_send, rs_recv, top_send, top_recv, ag_send, ag_recv,
 ):
     me = lax.axis_index("row")
     steps = (0, 1, n - 1, 4, n - 4, 5, n - 5, n // 2)
@@ -53,20 +54,90 @@
         greeted += [(me + o) % n for o in steps[1:]] + [(me + SUB * q) % n for q in range(1, subs)]
     for p in greeted:
         pl.semaphore_signal(barrier, inc=1, device_id=at(p), device_id_type=pl.DeviceIdType.MESH)
-    own_copy = pltpu.make_async_copy(basis, shard.at[0], loc_sem.at[0])
+    relayed = n == SUB
+    z, q = me // 4, me % 4
+    own_slot = z if relayed else 0
+    own_copy = pltpu.make_async_copy(basis, shard.at[own_slot], loc_sem.at[0])
     own_copy.start()
+    small = [
+        pltpu.make_async_copy(x, y, loc_sem.at[2 + i])
+        for i, (x, y) in enumerate(((springs_in, springs), (rows_in, rows), (owner_in, owner), (offset_in, offset)))
+    ]
+    for c in small:
+        c.start()
     tang_copy = pltpu.make_async_copy(tangent, tang, loc_sem.at[1])
     tang_copy.start()
     pl.semaphore_wait(barrier, len(greeted))
 
+    def remote(src, dst, s_sem, r_sem, p):
+        return pltpu.make_async_remote_copy(
+            src, dst, s_sem, r_sem, device_id=at(p), device_id_type=pl.DeviceIdType.MESH
+        )
+
+    def up(h):
+        src = basis if h == 0 else shard.at[(z - h) % 4]
+        return remote(src, shard.at[(z - h) % 4], up_send.at[h], up_recv.at[h], (me + 4) % n)
+
+    def down(h):
+        src = basis if h == 0 else shard.at[(z + h) % 4]
+        return remote(src, shard.at[(z + h) % 4], down_send.at[h], down_recv.at[h], (me + n - 4) % n)
+
+    first, last = jnp.where(q == 0, 1, 0), jnp.where(q == 3, 1, 0)
+    gives = (
+        (4, (z + first) % 4, z * 4 + (q + 3) % 4),
+        (5, (z + 1 + first) % 4, z * 4 + (q + 3) % 4),
+        (6, (z + 4 - last) % 4, z * 4 + (q + 1) % 4),
+        (7, (z + 3 - last) % 4, z * 4 + (q + 1) % 4),
+    )
+
+    def give(h):
+        for slot_id, whose, p in gives:
+            far = jnp.where(whose < z, z - whose, whose - z)
+
+            @pl.when(far == h)
+            def _(slot_id=slot_id, whose=whose, p=p):
+                src = basis if h == 0 else shard.at[whose]
+                remote(src, shard.at[slot_id], send_sem.at[slot_id], recv_sem.at[slot_id], p).start()
+
+    def hop(h):
+        @pl.when(z >= h)
+        def _():
+            up(h - 1).wait_recv()
+
+        if h < 3:
+            @pl.when((z >= h) & (z < 3))
+            def _():
+                up(h).start()
+
+        @pl.when(z + h <= 3)
+        def _():
+            down(h - 1).wait_recv()
+
+        if h < 3:
+            @pl.when((z + h <= 3) & (z > 0))
+            def _():
+                down(h).start()
+
+        give(h)
+
     sends = []
-    for k in (7, 5, 6, 3, 4, 1, 2):
-        c = pltpu.make_async_remote_copy(
-            basis, shard.at[k], send_sem.at[k], recv_sem.at[k],
-            device_id=at((me + n - steps[k]) % n), device_id_type=pl.DeviceIdType.MESH,
-        )
-        c.start()
-        sends.append((k, c))
+    if relayed:
+        @pl.when(z < 3)
+        def _():
+            up(0).start()
+
+        @pl.when(z > 0)
+        def _():
+            down(0).start()
+
+        give(0)
+    else:
+        for k in (7, 5, 6, 3, 4, 1, 2):
+            c = remote(basis, shard.at[k], send_sem.at[k], recv_sem.at[k], (me + n - steps[k]) % n)
+            c.start()
+            sends.append(c)
+    for c in small:
+        c.wait()
 
     away = owner[...] - me
     away = jnp.where(away < 0, away + n, away)
@@ -103,10 +174,15 @@
             dense_lo[at_row, cp * 128:(cp + 1) * 128] = lo
         return 0
 
-    lax.fori_loop(0, 16, build, 0)
+    lax.fori_loop(0, 6, build, 0)
+    if relayed:
+        hop(1)
+    lax.fori_loop(6, 16, build, 0)
+    if relayed:
+        hop(2)
 
     own_copy.wait()
-    own = shard[0]
+    own = shard[own_slot]
     t_hi, t_lo = split(own.T)
     eye = p_ids == lane
     spring = jnp.concatenate(
@@ -120,9 +196,16 @@
         return mm3(dense_hi[:, ks], dense_lo[:, ks], g_hi, g_lo)
 
     total = term(0, own)
-    for k in (1, 2, 3, 4, 5, 6, 7):
-        pltpu.make_async_copy(shard.at[k], shard.at[k], recv_sem.at[k]).wait()
-        total = total + term(k, shard[k])
+    if relayed:
+        hop(3)
+        for k, ahead in ((3, 1), (4, 3), (7, 2)):
+            total = total + term(k, shard[(z + ahead) % 4])
+        order = ((1, 4), (2, 6), (5, 5), (6, 7))
+    else:
+        order = [(k, k) for k in range(1, 8)]
+    for k, slot_id in order:
+        remote(basis, shard.at[slot_id], send_sem.at[slot_id], recv_sem.at[slot_id], mate(1)).wait_recv()
+        total = total + term(k, shard[slot_id])
     acc[...] = total
     image = scaled + jnp.concatenate([acc[pl.ds(r, B, stride=BR_DEV), :] for r in range(BR_DEV)], axis=0)
     stiff[...] = image
@@ -168,7 +251,21 @@
     for c in ag:
         c.wait_recv()
     reduced[...] = red[...].reshape(MODES, MODES)
-    for k, c in sends:
+    if relayed:
+        for h in range(3):
+            @pl.when((z >= h) & (z < 3))
+            def _(h=h):
+                up(h).wait_send()
+
+            @pl.when((z + h <= 3) & (z > 0))
+            def _(h=h):
+                down(h).wait_send()
+
+        for slot_id in range(4, 8):
+            remote(
+                basis, shard.at[slot_id], send_sem.at[slot_id], recv_sem.at[slot_id], mate(1)
+            ).wait_send()
+    for c in sends:
         c.wait_send()
     for c in rs + ag:
         c.wait_send()
@@ -189,9 +286,13 @@
             jax.ShapeDtypeStruct((BR_DEV * B, MODES), F32),
             jax.ShapeDtypeStruct((MODES, MODES), F32),
         ),
-        in_specs=[hbm, vm, hbm, vm, vm, vm, pl.BlockSpec(memory_space=pltpu.SMEM)],
+        in_specs=[hbm] * 6 + [pl.BlockSpec(memory_space=pltpu.SMEM)],
         out_specs=(vm, vm),
         scratch_shapes=[
+            pltpu.VMEM((2, MODES), F32),
+            pltpu.VMEM((1, CAP), jnp.int32),
+            pltpu.VMEM((1, CAP), jnp.int32),
+            pltpu.VMEM((1, CAP), jnp.int32),
             pltpu.VMEM((8, BR_DEV * B, MODES), F32),
             pltpu.VMEM((CAP, B * B), F32),
             pltpu.VMEM((BR_DEV * B, 32 * B), BF16),
@@ -201,9 +302,13 @@
             pltpu.VMEM((SUB, 8, MODES), F32),
             pltpu.VMEM((subs, 8, MODES), F32),
             pltpu.VMEM((SUB, 8, MODES), F32),
-            pltpu.SemaphoreType.DMA((2,)),
+            pltpu.SemaphoreType.DMA((6,)),
             pltpu.SemaphoreType.DMA((8,)),
             pltpu.SemaphoreType.DMA((8,)),
+            pltpu.SemaphoreType.DMA((3,)),
+            pltpu.SemaphoreType.DMA((3,)),
+            pltpu.SemaphoreType.DMA((3,)),
+            pltpu.SemaphoreType.DMA((3,)),
             pltpu.SemaphoreType.DMA((SUB,)),
             pltpu.SemaphoreType.DMA((SUB,)),
             pltpu.SemaphoreType.DMA((subs,)),
@@ -212,7 +317,7 @@
             pltpu.SemaphoreType.DMA((SUB,)),
         ],
         compiler_params=pltpu.CompilerParams(
-            collective_id=0, has_side_effects=True, vmem_limit_bytes=32 * 1024 * 1024
+            collective_id=0, has_side_effects=True, vmem_limit_bytes=60 * 1024 * 1024
         ),
     )(
         basis, springs.reshape(2, MODES), tangent_blocks,

time: 45.1 us -> 37 us (0.82)
  Pallas kernels: 37.2 us -> 32.5 us
  local copies, waits for them, and re-layouts: 6.42 us -> 3.04 us
    pallas_call x1, Pallas kernels: 37.2 us -> 32.5 us  [shards(): pl.pallas_call(functools.partial(kernel, n, dof_total), out_shape=(jax.Sh...]
    unnamed x14 -> x2, local copies, waits for them, and re-layouts: 6.42 us -> 3.04 us
where the time goes in v2:
time: 37 us; the launch traced here: 36.8 us
  Pallas kernels  32.5 us (88%)
  local copies, waits for them, and re-layouts  3.04 us (8%)
  between operations  1.29 us (3%)
    pallas_call x1, Pallas kernels, shards(): pl.pallas_call(functools.partial(kernel, n, dof_total), out_shape=(jax.Sh...  32.5 us
    unnamed x2, local copies, waits for them, and re-layouts  3.04 us

profile of v2, /device:TPU:0, one launch (start us, length us, event | category | flops | bytes accessed | tf_op | source)
XLA Modules:
  0.0 36.8 jit_solution(9848979397581792471)
XLA Ops:
  1.3 32.5 %shard_map.86 = (f32[256,128]{1,0:T(8,128)}, f32[128,128]{1,0:T(8,128)}) custom-call(f32[256,128]{1,0:T(8,128)} %basis.1, f32[2,128]{1,0:T(2,128)} %bitcast.4, f32[128,4096]{1,0:T(8,128)} %tangent.1, s32[1,128]{1,0:T(1,128)} %bitcast.5, s32[1,128]{1,0:T(1,128)} %bitcast.6, s32[1,128]{1,0:T(1,128)} %bitcast.7, s32[1]{0:T(128)S(6)} %copy.11.count), custom_call_target="tpu_custom_call" | custom-call | tf_op jit(solution)/shard_map/pallas_call | solution.py:283
  33.8 1.6 %copy.12 = f32[256,128]{1,0:T(8,128)} copy(f32[256,128]{1,0:T(8,128)} %get-tuple-element.4) | data formatting | bytes 262144
  35.3 1.5 %copy.13 = f32[128,128]{1,0:T(8,128)} copy(f32[128,128]{1,0:T(8,128)} %get-tuple-element.5) | data formatting | bytes 131072

commit v3 on v2

--- a/solution.py
+++ b/solution.py
@@ -11,7 +11,6 @@
 MODES = 128
 BR_DEV = 4
 CAP = 128
-SUB = 16
 F32, BF16 = jnp.float32, jnp.bfloat16
 
 
@@ -39,23 +38,22 @@
 ):
     me = lax.axis_index("row")
     steps = (0, 1, n - 1, 4, n - 4, 5, n - 5, n // 2)
-    subs = n // SUB
-    sub, pos = me // SUB, me % SUB
+    planes = n // 4
+    z, q = me // 4, me % 4
+    relayed = n == 16
 
     def at(p):
         return {"row": p}
 
     def mate(s):
-        return sub * SUB + (pos + s) % SUB
+        return z * 4 + (q + s) % 4
 
     barrier = pltpu.get_barrier_semaphore()
-    greeted = [mate(s) for s in range(1, SUB)]
-    if subs > 1:
-        greeted += [(me + o) % n for o in steps[1:]] + [(me + SUB * q) % n for q in range(1, subs)]
+    greeted = [mate(s) for s in range(1, 4)] + [(me + 4 * s) % n for s in range(1, planes)]
+    if not relayed:
+        greeted += [(me + o) % n for o in steps[1:]]
     for p in greeted:
         pl.semaphore_signal(barrier, inc=1, device_id=at(p), device_id_type=pl.DeviceIdType.MESH)
-    relayed = n == SUB
-    z, q = me // 4, me % 4
     own_slot = z if relayed else 0
     own_copy = pltpu.make_async_copy(basis, shard.at[own_slot], loc_sem.at[0])
     own_copy.start()
@@ -74,13 +72,21 @@
             src, dst, s_sem, r_sem, device_id=at(p), device_id_type=pl.DeviceIdType.MESH
         )
 
-    def up(h):
-        src = basis if h == 0 else shard.at[(z - h) % 4]
-        return remote(src, shard.at[(z - h) % 4], up_send.at[h], up_recv.at[h], (me + 4) % n)
-
-    def down(h):
-        src = basis if h == 0 else shard.at[(z + h) % 4]
-        return remote(src, shard.at[(z + h) % 4], down_send.at[h], down_recv.at[h], (me + n - 4) % n)
+    def half(ref, c):
+        return ref.at[pl.ds(c * 128, 128)]
+
+    def up(h, c):
+        to = half(shard.at[(z - h) % 4], c)
+        return remote(half(basis, c) if h == 0 else to, to, up_send.at[h, c], up_recv.at[h, c], (me + 4) % n)
+
+    def down(h, c):
+        to = half(shard.at[(z + h) % 4], c)
+        return remote(half(basis, c) if h == 0 else to, to, down_send.at[h, c], down_recv.at[h, c], (me + n - 4) % n)
+
+    def handed(src, slot_id, c, p):
+        return remote(
+            half(src, c), half(shard.at[slot_id], c), send_sem.at[slot_id, c], recv_sem.at[slot_id, c], p
+        )
 
     first, last = jnp.where(q == 0, 1, 0), jnp.where(q == 3, 1, 0)
     gives = (
@@ -90,50 +96,52 @@
         (7, (z + 3 - last) % 4, z * 4 + (q + 1) % 4),
     )
 
-    def give(h):
+    def give(h, c):
         for slot_id, whose, p in gives:
             far = jnp.where(whose < z, z - whose, whose - z)
 
             @pl.when(far == h)
             def _(slot_id=slot_id, whose=whose, p=p):
-                src = basis if h == 0 else shard.at[whose]
-                remote(src, shard.at[slot_id], send_sem.at[slot_id], recv_sem.at[slot_id], p).start()
+                handed(basis if h == 0 else shard.at[whose], slot_id, c, p).start()
 
     def hop(h):
-        @pl.when(z >= h)
-        def _():
-            up(h - 1).wait_recv()
-
-        if h < 3:
-            @pl.when((z >= h) & (z < 3))
+        for c in range(2):
+            @pl.when(z >= h)
             def _():
-                up(h).start()
-
-        @pl.when(z + h <= 3)
-        def _():
-            down(h - 1).wait_recv()
-
-        if h < 3:
-            @pl.when((z + h <= 3) & (z > 0))
+                up(h - 1, c).wait_recv()
+
+            if h < 3:
+                @pl.when((z >= h) & (z < 3))
+                def _():
+                    up(h, c).start()
+
+            @pl.when(z + h <= 3)
             def _():
-                down(h).start()
-
-        give(h)
+                down(h - 1, c).wait_recv()
+
+            if h < 3:
+                @pl.when((z + h <= 3) & (z > 0))
+                def _():
+                    down(h, c).start()
+
+            give(h, c)
 
     sends = []
     if relayed:
-        @pl.when(z < 3)
-        def _():
-            up(0).start()
-
-        @pl.when(z > 0)
-        def _():
-            down(0).start()
-
-        give(0)
+        for c in range(2):
+            @pl.when(z < 3)
+            def _():
+                up(0, c).start()
+
+            @pl.when(z > 0)
+            def _():
+                down(0, c).start()
+
+        for c in range(2):
+            give(0, c)
     else:
-        for k in (7, 5, 6, 3, 4, 1, 2):
-            c = remote(basis, shard.at[k], send_sem.at[k], recv_sem.at[k], (me + n - steps[k]) % n)
+        for k in range(1, 8):
+            c = remote(basis, shard.at[k], send_sem.at[k, 0], recv_sem.at[k, 0], (me + n - steps[k]) % n)
             c.start()
             sends.append(c)
     for c in small:
@@ -204,74 +212,60 @@
     else:
         order = [(k, k) for k in range(1, 8)]
     for k, slot_id in order:
-        remote(basis, shard.at[slot_id], send_sem.at[slot_id], recv_sem.at[slot_id], mate(1)).wait_recv()
+        if relayed:
+            for c in range(2):
+                handed(basis, slot_id, c, mate(1)).wait_recv()
+        else:
+            sends[k - 1].wait_recv()
         total = total + term(k, shard[slot_id])
     acc[...] = total
     image = scaled + jnp.concatenate([acc[pl.ds(r, B, stride=BR_DEV), :] for r in range(BR_DEV)], axis=0)
     stiff[...] = image
     i_hi, i_lo = split(image)
-    part[...] = (mm3(t_hi, t_lo, i_hi, i_lo) * (1.0 / dof_total)).reshape(SUB, 8, MODES)
-
-    rs = []
-    for s in range(1, SUB):
-        c = pltpu.make_async_remote_copy(
-            part.at[(pos + s) % SUB], rs_buf.at[s], rs_send.at[s], rs_recv.at[s],
-            device_id=at(mate(s)), device_id_type=pl.DeviceIdType.MESH,
-        )
+    part[...] = (mm3(t_hi, t_lo, i_hi, i_lo) * (1.0 / dof_total)).reshape(4, MODES // 4, MODES)
+
+    rs = [remote(part.at[(q + s) % 4], rs_buf.at[s], rs_send.at[s], rs_recv.at[s], mate(s)) for s in range(1, 4)]
+    for c in rs:
         c.start()
-        rs.append(c)
-    mine = part[pos]
-    for s in range(1, SUB):
+    mine = part[q]
+    for s in range(1, 4):
         rs[s - 1].wait_recv()
         mine = mine + rs_buf[s]
-    if subs > 1:
-        top_buf[sub] = mine
-        top = []
-        for q in range(1, subs):
-            c = pltpu.make_async_remote_copy(
-                top_buf.at[sub], top_buf.at[sub], top_send.at[q], top_recv.at[q],
-                device_id=at((me + SUB * q) % n), device_id_type=pl.DeviceIdType.MESH,
-            )
-            c.start()
-            top.append(c)
-        for c in top:
-            c.wait_recv()
-        mine = top_buf[0]
-        for q in range(1, subs):
-            mine = mine + top_buf[q]
-    red[pos] = mine
-    ag = []
-    for s in range(1, SUB):
-        c = pltpu.make_async_remote_copy(
-            red.at[pos], red.at[pos], ag_send.at[s], ag_recv.at[s],
-            device_id=at(mate(s)), device_id_type=pl.DeviceIdType.MESH,
-        )
+    top_buf[z] = mine
+    top = [
+        remote(top_buf.at[z], top_buf.at[z], top_send.at[s], top_recv.at[s], (me + 4 * s) % n)
+        for s in range(1, planes)
+    ]
+    for c in top:
         c.start()
-        ag.append(c)
+    for c in top:
+        c.wait_recv()
+    mine = top_buf[0]
+    for s in range(1, planes):
+        mine = mine + top_buf[s]
+    red[q] = mine
+    ag = [remote(red.at[q], red.at[q], ag_send.at[s], ag_recv.at[s], mate(s)) for s in range(1, 4)]
+    for c in ag:
+        c.start()
     for c in ag:
         c.wait_recv()
     reduced[...] = red[...].reshape(MODES, MODES)
     if relayed:
-        for h in range(3):
+        for h, c in [(h, c) for h in range(3) for c in range(2)]:
             @pl.when((z >= h) & (z < 3))
-            def _(h=h):
-                up(h).wait_send()
+            def _(h=h, c=c):
+                up(h, c).wait_send()
 
             @pl.when((z + h <= 3) & (z > 0))
-            def _(h=h):
-                down(h).wait_send()
-
-        for slot_id in range(4, 8):
-            remote(
-                basis, shard.at[slot_id], send_sem.at[slot_id], recv_sem.at[slot_id], mate(1)
-            ).wait_send()
+            def _(h=h, c=c):
+                down(h, c).wait_send()
+
+        for slot_id, c in [(i, c) for i in range(4, 8) for c in range(2)]:
+            handed(basis, slot_id, c, mate(1)).wait_send()
     for c in sends:
         c.wait_send()
-    for c in rs + ag:
+    for c in rs + top + ag:
         c.wait_send()
-    if subs > 1:
-        for c in top:
-            c.wait_send()
 
 
 def shards(basis, springs, tangent_blocks, tile_rows, tile_owner, tile_offset, tile_count):
@@ -279,7 +273,7 @@
     dof_total = basis.shape[0] * n
     vm = pl.BlockSpec(memory_space=pltpu.VMEM)
     hbm = pl.BlockSpec(memory_space=pl.ANY)
-    subs = max(n // SUB, 2)
+    planes = n // 4
     return pl.pallas_call(
         functools.partial(kernel, n, dof_total),
         out_shape=(
@@ -298,23 +292,23 @@
             pltpu.VMEM((BR_DEV * B, 32 * B), BF16),
             pltpu.VMEM((BR_DEV * B, 32 * B), BF16),
             pltpu.VMEM((BR_DEV * B, MODES), F32),
-            pltpu.VMEM((SUB, 8, MODES), F32),
-            pltpu.VMEM((SUB, 8, MODES), F32),
-            pltpu.VMEM((subs, 8, MODES), F32),
-            pltpu.VMEM((SUB, 8, MODES), F32),
+            pltpu.VMEM((4, MODES // 4, MODES), F32),
+            pltpu.VMEM((4, MODES // 4, MODES), F32),
+            pltpu.VMEM((planes, MODES // 4, MODES), F32),
+            pltpu.VMEM((4, MODES // 4, MODES), F32),
             pltpu.SemaphoreType.DMA((6,)),
-            pltpu.SemaphoreType.DMA((8,)),
-            pltpu.SemaphoreType.DMA((8,)),
-            pltpu.SemaphoreType.DMA((3,)),
-            pltpu.SemaphoreType.DMA((3,)),
-            pltpu.SemaphoreType.DMA((3,)),
-            pltpu.SemaphoreType.DMA((3,)),
-            pltpu.SemaphoreType.DMA((SUB,)),
-            pltpu.SemaphoreType.DMA((SUB,)),
-            pltpu.SemaphoreType.DMA((subs,)),
-            pltpu.SemaphoreType.DMA((subs,)),
-            pltpu.SemaphoreType.DMA((SUB,)),
-            pltpu.SemaphoreType.DMA((SUB,)),
+            pltpu.SemaphoreType.DMA((8, 2)),
+            pltpu.SemaphoreType.DMA((8, 2)),
+            pltpu.SemaphoreType.DMA((3, 2)),
+            pltpu.SemaphoreType.DMA((3, 2)),
+            pltpu.SemaphoreType.DMA((3, 2)),
+            pltpu.SemaphoreType.DMA((3, 2)),
+            pltpu.SemaphoreType.DMA((4,)),
+            pltpu.SemaphoreType.DMA((4,)),
+            pltpu.SemaphoreType.DMA((planes,)),
+            pltpu.SemaphoreType.DMA((planes,)),
+            pltpu.SemaphoreType.DMA((4,)),
+            pltpu.SemaphoreType.DMA((4,)),
         ],
         compiler_params=pltpu.CompilerParams(
             collective_id=0, has_side_effects=True, vmem_limit_bytes=60 * 1024 * 1024

time: 37 us -> 34.7 us (0.938)
  Pallas kernels: 32.5 us -> 30.2 us
    pallas_call x1, Pallas kernels: 32.5 us -> 30.2 us  [shards(): pl.pallas_call(functools.partial(kernel, n, dof_total), out_shape=(jax.Sh...]
where the time goes in v3:
time: 34.7 us; the launch traced here: 34.5 us
  Pallas kernels  30.2 us (87%)
  local copies, waits for them, and re-layouts  3.04 us (9%)
  between operations  1.29 us (4%)
    pallas_call x1, Pallas kernels, shards(): pl.pallas_call(functools.partial(kernel, n, dof_total), out_shape=(jax.Sh...  30.2 us
    unnamed x2, local copies, waits for them, and re-layouts  3.04 us

profile of v3, /device:TPU:0, one launch (start us, length us, event | category | flops | bytes accessed | tf_op | source)
XLA Modules:
  0.0 34.5 jit_solution(10063342144584880388)
XLA Ops:
  1.3 30.2 %shard_map.86 = (f32[256,128]{1,0:T(8,128)}, f32[128,128]{1,0:T(8,128)}) custom-call(f32[256,128]{1,0:T(8,128)} %basis.1, f32[2,128]{1,0:T(2,128)} %bitcast.4, f32[128,4096]{1,0:T(8,128)} %tangent.1, s32[1,128]{1,0:T(1,128)} %bitcast.5, s32[1,128]{1,0:T(1,128)} %bitcast.6, s32[1,128]{1,0:T(1,128)} %bitcast.7, s32[1]{0:T(128)S(6)} %copy.11.count), custom_call_target="tpu_custom_call" | custom-call | tf_op jit(solution)/shard_map/pallas_call | solution.py:277
  31.5 1.6 %copy.12 = f32[256,128]{1,0:T(8,128)} copy(f32[256,128]{1,0:T(8,128)} %get-tuple-element.4) | data formatting | bytes 262144
  33.0 1.5 %copy.13 = f32[128,128]{1,0:T(8,128)} copy(f32[128,128]{1,0:T(8,128)} %get-tuple-element.5) | data formatting | bytes 131072

commit v4 on v3

--- a/solution.py
+++ b/solution.py
@@ -11,6 +11,8 @@
 MODES = 128
 BR_DEV = 4
 CAP = 128
+PIECES = 4
+PIECE = BR_DEV * B // PIECES
 F32, BF16 = jnp.float32, jnp.bfloat16
 
 
@@ -30,10 +32,10 @@
 
 def kernel(
     n, dof_total,
-    basis, springs_in, tangent, rows_in, owner_in, offset_in, count,
+    basis, springs_in, tangent, rows_in, owner_in, offset_in, count_in,
     stiff, reduced,
-    springs, rows, owner, offset,
-    shard, tang, dense_hi, dense_lo, acc, part, rs_buf, top_buf, red,
+    springs, rows, owner, offset, count,
+    shard, tang, dense_hi, dense_lo, acc, acc2, part, rs_buf, top_buf, red,
     loc_sem, send_sem, recv_sem, up_send, up_recv, down_send, down_recv, rs_send, rs_recv, top_send, top_recv, ag_send, ag_recv,
 ):
     me = lax.axis_index("row")
@@ -59,7 +61,7 @@
     own_copy.start()
     small = [
         pltpu.make_async_copy(x, y, loc_sem.at[2 + i])
-        for i, (x, y) in enumerate(((springs_in, springs), (rows_in, rows), (owner_in, owner), (offset_in, offset)))
+        for i, (x, y) in enumerate(((springs_in, springs), (rows_in, rows), (owner_in, owner), (offset_in, offset), (count_in, count)))
     ]
     for c in small:
         c.start()
@@ -72,20 +74,20 @@
             src, dst, s_sem, r_sem, device_id=at(p), device_id_type=pl.DeviceIdType.MESH
         )
 
-    def half(ref, c):
-        return ref.at[pl.ds(c * 128, 128)]
+    def piece(ref, c):
+        return ref.at[pl.ds(c * PIECE, PIECE)]
 
     def up(h, c):
-        to = half(shard.at[(z - h) % 4], c)
-        return remote(half(basis, c) if h == 0 else to, to, up_send.at[h, c], up_recv.at[h, c], (me + 4) % n)
+        to = piece(shard.at[(z - h) % 4], c)
+        return remote(piece(basis, c) if h == 0 else to, to, up_send.at[h, c], up_recv.at[h, c], (me + 4) % n)
 
     def down(h, c):
-        to = half(shard.at[(z + h) % 4], c)
-        return remote(half(basis, c) if h == 0 else to, to, down_send.at[h, c], down_recv.at[h, c], (me + n - 4) % n)
+        to = piece(shard.at[(z + h) % 4], c)
+        return remote(piece(basis, c) if h == 0 else to, to, down_send.at[h, c], down_recv.at[h, c], (me + n - 4) % n)
 
     def handed(src, slot_id, c, p):
         return remote(
-            half(src, c), half(shard.at[slot_id], c), send_sem.at[slot_id, c], recv_sem.at[slot_id, c], p
+            piece(src, c), piece(shard.at[slot_id], c), send_sem.at[slot_id, c], recv_sem.at[slot_id, c], p
         )
 
     first, last = jnp.where(q == 0, 1, 0), jnp.where(q == 3, 1, 0)
@@ -105,7 +107,7 @@
                 handed(basis if h == 0 else shard.at[whose], slot_id, c, p).start()
 
     def hop(h):
-        for c in range(2):
+        for c in range(PIECES):
             @pl.when(z >= h)
             def _():
                 up(h - 1, c).wait_recv()
@@ -128,7 +130,7 @@
 
     sends = []
     if relayed:
-        for c in range(2):
+        for c in range(PIECES):
             @pl.when(z < 3)
             def _():
                 up(0, c).start()
@@ -137,7 +139,7 @@
             def _():
                 down(0, c).start()
 
-        for c in range(2):
+        for c in range(PIECES):
             give(0, c)
     else:
         for k in range(1, 8):
@@ -213,14 +215,16 @@
         order = [(k, k) for k in range(1, 8)]
     for k, slot_id in order:
         if relayed:
-            for c in range(2):
+            for c in range(PIECES):
                 handed(basis, slot_id, c, mate(1)).wait_recv()
         else:
             sends[k - 1].wait_recv()
         total = total + term(k, shard[slot_id])
     acc[...] = total
     image = scaled + jnp.concatenate([acc[pl.ds(r, B, stride=BR_DEV), :] for r in range(BR_DEV)], axis=0)
-    stiff[...] = image
+    acc2[...] = image
+    out_copy = pltpu.make_async_copy(acc2, stiff, loc_sem.at[0])
+    out_copy.start()
     i_hi, i_lo = split(image)
     part[...] = (mm3(t_hi, t_lo, i_hi, i_lo) * (1.0 / dof_total)).reshape(4, MODES // 4, MODES)
 
@@ -250,8 +254,9 @@
     for c in ag:
         c.wait_recv()
     reduced[...] = red[...].reshape(MODES, MODES)
-    if relayed:
-        for h, c in [(h, c) for h in range(3) for c in range(2)]:
+    out_copy.wait()
+    if relayed:
+        for h, c in [(h, c) for h in range(3) for c in range(PIECES)]:
             @pl.when((z >= h) & (z < 3))
             def _(h=h, c=c):
                 up(h, c).wait_send()
@@ -260,7 +265,7 @@
             def _(h=h, c=c):
                 down(h, c).wait_send()
 
-        for slot_id, c in [(i, c) for i in range(4, 8) for c in range(2)]:
+        for slot_id, c in [(i, c) for i in range(4, 8) for c in range(PIECES)]:
             handed(basis, slot_id, c, mate(1)).wait_send()
     for c in sends:
         c.wait_send()
@@ -280,29 +285,31 @@
             jax.ShapeDtypeStruct((BR_DEV * B, MODES), F32),
             jax.ShapeDtypeStruct((MODES, MODES), F32),
         ),
-        in_specs=[hbm] * 6 + [pl.BlockSpec(memory_space=pltpu.SMEM)],
-        out_specs=(vm, vm),
+        in_specs=[hbm] * 7,
+        out_specs=(hbm, vm),
         scratch_shapes=[
             pltpu.VMEM((2, MODES), F32),
             pltpu.VMEM((1, CAP), jnp.int32),
             pltpu.VMEM((1, CAP), jnp.int32),
             pltpu.VMEM((1, CAP), jnp.int32),
+            pltpu.SMEM((1,), jnp.int32),
             pltpu.VMEM((8, BR_DEV * B, MODES), F32),
             pltpu.VMEM((CAP, B * B), F32),
             pltpu.VMEM((BR_DEV * B, 32 * B), BF16),
             pltpu.VMEM((BR_DEV * B, 32 * B), BF16),
             pltpu.VMEM((BR_DEV * B, MODES), F32),
+            pltpu.VMEM((BR_DEV * B, MODES), F32),
             pltpu.VMEM((4, MODES // 4, MODES), F32),
             pltpu.VMEM((4, MODES // 4, MODES), F32),
             pltpu.VMEM((planes, MODES // 4, MODES), F32),
             pltpu.VMEM((4, MODES // 4, MODES), F32),
-            pltpu.SemaphoreType.DMA((6,)),
-            pltpu.SemaphoreType.DMA((8, 2)),
-            pltpu.SemaphoreType.DMA((8, 2)),
-            pltpu.SemaphoreType.DMA((3, 2)),
-            pltpu.SemaphoreType.DMA((3, 2)),
-            pltpu.SemaphoreType.DMA((3, 2)),
-            pltpu.SemaphoreType.DMA((3, 2)),
+            pltpu.SemaphoreType.DMA((7,)),
+            pltpu.SemaphoreType.DMA((8, PIECES)),
+            pltpu.SemaphoreType.DMA((8, PIECES)),
+            pltpu.SemaphoreType.DMA((3, PIECES)),
+            pltpu.SemaphoreType.DMA((3, PIECES)),
+            pltpu.SemaphoreType.DMA((3, PIECES)),
+            pltpu.SemaphoreType.DMA((3, PIECES)),
             pltpu.SemaphoreType.DMA((4,)),
             pltpu.SemaphoreType.DMA((4,)),
             pltpu.SemaphoreType.DMA((planes,)),

time: 34.7 us -> 34.5 us (level)
  no operation moved by 1% of the time
where the time goes in v4:
time: 34.5 us; the launch traced here: 34.3 us
  Pallas kernels  30 us (87%)
  local copies, waits for them, and re-layouts  3.04 us (9%)
  between operations  1.29 us (4%)
    pallas_call x1, Pallas kernels, shards(): pl.pallas_call(functools.partial(kernel, n, dof_total), out_shape=(jax.Sh...  30 us
    unnamed x2, local copies, waits for them, and re-layouts  3.04 us

profile of v4, /device:TPU:0, one launch (start us, length us, event | category | flops | bytes accessed | tf_op | source)
XLA Modules:
  0.0 34.3 jit_solution(2197291133666877502)
XLA Ops:
  1.3 30.0 %shard_map.86 = (f32[256,128]{1,0:T(8,128)}, f32[128,128]{1,0:T(8,128)}) custom-call(f32[256,128]{1,0:T(8,128)} %basis.1, f32[2,128]{1,0:T(2,128)} %bitcast.4, f32[128,4096]{1,0:T(8,128)} %tangent.1, s32[1,128]{1,0:T(1,128)} %bitcast.5, s32[1,128]{1,0:T(1,128)} %bitcast.6, s32[1,128]{1,0:T(1,128)} %bitcast.7, s32[1]{0:T(128)S(6)} %copy.11.count_in), custom_call_target="tpu_custom_call" | custom-call | tf_op jit(solution)/shard_map/pallas_call | solution.py:282
  31.3 1.6 %copy.12 = f32[256,128]{1,0:T(8,128)} copy(f32[256,128]{1,0:T(8,128)} %get-tuple-element.4) | data formatting | bytes 262144
  32.9 1.5 %copy.13 = f32[128,128]{1,0:T(8,128)} copy(f32[128,128]{1,0:T(8,128)} %get-tuple-element.5) | data formatting | bytes 131072
